TPU v7x, 128 devices: a whole 4x4x4 slice. The times are simulated.
128 devices in a mesh: expert: 32 (over y, z, core), shard: 4 (over x).
Axes of the slice: x: 4, y: 4, z: 4, core: 2. Of those that a mesh axis runs over, the one named last changes fastest.
Arguments:
- tokens: bfloat16 [16384, 768], P(('expert', 'shard')), may hold values from -6 to 6
- seq_lengths: int32 [128, 4], P(('expert', 'shard')), may hold values from 1 to 96, 128 in all within a row
- routes: int32 [16384, 2], P(('expert', 'shard')), may hold values from 0 to 63, all different within a row; in each aligned block of 128 rows (0 to 127, 128 to 255, ...) at most 6 rows name the same one
- gain_attn: bfloat16 [768], P('shard'), may hold values from 0.25 to 1.75
- w_query: bfloat16 [768, 768], P('shard'), may hold values from -0.21875 to 0.21875
- w_key: bfloat16 [768, 768], P('shard'), may hold values from -0.21875 to 0.21875
- w_value: bfloat16 [768, 768], P('shard'), may hold values from -0.21875 to 0.21875
- w_output: bfloat16 [768, 768], P('shard'), may hold values from -0.875 to 0.875
- rel_bias: bfloat16 [12, 32], P('shard'), may hold values from -3 to 3
- gain_moe: bfloat16 [768], P('shard'), may hold values from 0.25 to 1.75
- w_router: bfloat16 [768, 64], P('shard'), may hold values from -0.21875 to 0.21875
- w_in: bfloat16 [64, 768, 3072], P('expert', None, 'shard'), may hold values from -0.21875 to 0.21875
- w_out: bfloat16 [64, 3072, 768], P('expert', 'shard'), may hold values from -0.109375 to 0.109375
- cotangent: bfloat16 [16384, 768], P(('expert', 'shard')), may hold values from -6 to 6
Outputs:
- result: bfloat16 [16384, 768], P(('expert', 'shard'))
- grad_tokens: float32 [16384, 768], P(('expert', 'shard'))
- grad_gain_attn: float32 [768], P('shard')
- grad_w_query: float32 [768, 768], P('shard')
- grad_w_key: float32 [768, 768], P('shard')
- grad_w_value: float32 [768, 768], P('shard')
- grad_w_output: float32 [768, 768], P('shard')
- grad_rel_bias: float32 [12, 32], P('shard')
- grad_gain_moe: float32 [768], P('shard')
- grad_w_router: float32 [768, 64], P('shard')
- grad_w_in: float32 [64, 768, 3072], P('expert', None, 'shard')
- grad_w_out: float32 [64, 3072, 768], P('expert', 'shard')
Inputs may be any that keep to these rules, and one draw needn't show every extreme that they name: `seq_lengths`: each rank's 4 lengths sum to 128; its sequences lie one after another in its rows; the largest length is exactly 96. `routes`: each row names two different experts. Among the rows of one rank no expert is named more than 6 times, a bound that some block reaches.
All inputs are finite; a program needn't handle non-finite values.
Results may differ from a plain program's by a relative error of at most 0.025.
Values may be sent and summed in bfloat16 or wider, within the bound.
No kernel may reach another device: no remote copies, remote signals or barrier semaphores. Data moves between devices by JAX's collectives and lax.ppermute only.
A program may use at most 128 MiB of HBM per device.

v0:
```python
import math

import jax
import jax.numpy as jnp
from jax import lax
from jax.sharding import PartitionSpec as P

epsilon = 1e-06
bucket_edges = list(range(1, 17)) + [
    int(math.ceil(16.0 * 8.0 ** ((bucket_level - 16) / 16.0))) for bucket_level in range(17, 32)
]


def sent_together(arrays, axis, dim, along):
    widths = [math.prod(a.shape[along:]) for a in arrays]
    both = jnp.concatenate(
        [a.reshape(*a.shape[:along], w) for a, w in zip(arrays, widths)], axis=along
    )
    result = lax.all_gather(both, axis, axis=dim, tiled=True)
    tiles = jnp.split(result, [sum(widths[:k]) for k in range(1, len(widths))], axis=along)
    return tuple(
        (b.reshape(*result.shape[:along], *a.shape[along:]) for a, b in zip(arrays, tiles))
    )


def side_by_side(arrays, axis, dim, along):
    widths = [math.prod(a.shape[along:]) for a in arrays]
    both = jnp.concatenate(
        [a.reshape(*a.shape[:along], w) for a, w in zip(arrays, widths)], axis=along
    )
    result = lax.psum_scatter(both, axis, scatter_dimension=dim, tiled=True)
    tiles = jnp.split(result, [sum(widths[:k]) for k in range(1, len(widths))], axis=along)
    return tuple(
        (b.reshape(*result.shape[:along], *a.shape[along:]) for a, b in zip(arrays, tiles))
    )


def in_one(arrays, axis):
    ends = [0]
    for a in arrays:
        ends.append(ends[-1] + a.size)
    so_far = lax.psum(jnp.concatenate([a.ravel() for a in arrays]), axis)
    return tuple((so_far[b:e].reshape(a.shape) for a, b, e in zip(arrays, ends, ends[1:])))


def row_segments(lengths, row_count):
    sequence_ends = jnp.cumsum(lengths)
    positions = jnp.arange(row_count, dtype=jnp.int32)
    return jnp.sum((positions[:, None] >= sequence_ends[None, :]).astype(jnp.int32), axis=1)


def position_tables(row_count, bucket_count):
    positions = jnp.arange(row_count, dtype=jnp.int32)
    distance = positions[:, None] - positions[None, :]
    edge_values = jnp.array(bucket_edges, dtype=jnp.int32)
    bucket = jnp.sum((distance[:, :, None] >= edge_values).astype(jnp.int32), axis=2)
    onehot = (bucket[:, :, None] == jnp.arange(bucket_count, dtype=jnp.int32)).astype(jnp.bfloat16)
    return (distance, onehot)


def capacity_slots(route_block, expert_count):
    order_block = jnp.arange(route_block.shape[0], dtype=jnp.int32)
    named_rows = jnp.sum(
        (route_block[:, :, None] == jnp.arange(expert_count, dtype=jnp.int32)).astype(jnp.int32),
        axis=1,
    )
    earlier = (order_block[None, :] < order_block[:, None]).astype(jnp.int32)
    counts = jnp.dot(earlier, named_rows, preferred_element_type=jnp.int32)
    return jnp.take_along_axis(counts, route_block, axis=1)


def gelu_tanh(argument):
    return jax.nn.gelu(argument, approximate=True)


def rms_backward(grad_normed, normed, scale):
    return scale * (grad_normed - normed * jnp.mean(grad_normed * normed, axis=1, keepdims=True))


def to_owners(outgoing, expert_count, capacity, features):
    expert_ranks = lax.axis_size("expert")
    shard_ranks = lax.axis_size("shard")
    local_count = expert_count // expert_ranks
    blocks = outgoing.reshape(expert_count, capacity, features)
    fanned = jnp.broadcast_to(
        blocks.reshape(expert_ranks, 1, local_count, capacity, features),
        (expert_ranks, shard_ranks, local_count, capacity, features),
    )
    arrived = lax.all_to_all(
        fanned.reshape(expert_ranks * shard_ranks * local_count, capacity, features),
        ("expert", "shard"),
        split_axis=0,
        concat_axis=1,
        tiled=True,
    )
    return arrived


def from_owners(partial_rows, expert_count, capacity, features):
    expert_ranks = lax.axis_size("expert")
    shard_ranks = lax.axis_size("shard")
    local_count = expert_count // expert_ranks
    returned_rows = lax.all_to_all(
        partial_rows.astype(jnp.bfloat16),
        ("expert", "shard"),
        split_axis=1,
        concat_axis=0,
        tiled=True,
    ).astype(partial_rows.dtype)
    summed_rows = jnp.sum(
        returned_rows.reshape(expert_ranks, shard_ranks, local_count, capacity, features), axis=1
    ).astype(jnp.bfloat16)
    return summed_rows.reshape(expert_count * capacity, features)


def shards(
    tokens,
    seq_lengths,
    routes,
    gain_attn,
    w_query,
    w_key,
    w_value,
    w_output,
    rel_bias,
    gain_moe,
    w_router,
    w_in,
    w_out,
    cotangent,
):
    gathered = (
        *sent_together((gain_attn, w_query, w_key, w_value, w_output), "shard", 0, 1),
        lax.all_gather(rel_bias, "shard", axis=0, tiled=True),
        *sent_together((gain_moe, w_router), "shard", 0, 1),
    )
    gain_one, query_w, key_w, value_w, output_w, bias_table, gain_two, router_w = gathered
    row_count, features = tokens.shape
    head_count, bucket_count = bias_table.shape
    head_size = features // head_count
    expert_count = router_w.shape[1]
    capacity = 3 * row_count // expert_count
    score_scale = 1.0 / math.sqrt(head_size)
    head_shape = (row_count, head_count, head_size)
    inputs = tokens.astype(jnp.float32)
    scale_one = lax.rsqrt(jnp.mean(inputs * inputs, axis=1, keepdims=True) + epsilon)
    normed_one = inputs * scale_one
    gain_one_f = gain_one.astype(jnp.float32)
    hidden_one = (normed_one * gain_one_f).astype(jnp.bfloat16)
    queries = jnp.dot(hidden_one, query_w, preferred_element_type=jnp.float32).astype(jnp.bfloat16)
    key_rows = jnp.dot(hidden_one, key_w, preferred_element_type=jnp.float32).astype(jnp.bfloat16)
    value_rows = jnp.dot(hidden_one, value_w, preferred_element_type=jnp.float32).astype(
        jnp.bfloat16
    )
    query_heads = queries.reshape(head_shape)
    key_heads = key_rows.reshape(head_shape)
    value_heads = value_rows.reshape(head_shape)
    segments = row_segments(seq_lengths[0], row_count)
    distance, onehot = position_tables(row_count, bucket_count)
    allowed = (segments[:, None] == segments[None, :]) & (distance >= 0)
    position_bias = jnp.einsum(
        "ijb,hb->hij", onehot, bias_table, preferred_element_type=jnp.float32
    )

    def scores_of():
        raw_scores = (
            jnp.einsum("ihd,jhd->hij", query_heads, key_heads, preferred_element_type=jnp.float32)
            * score_scale
            + position_bias
        )
        return jnp.where(allowed[None], raw_scores, -1000000000.0)

    scores = scores_of()
    row_max = jnp.max(scores, axis=2, keepdims=True)
    log_total = row_max + jnp.log(jnp.sum(jnp.exp(scores - row_max), axis=2, keepdims=True))
    attention = jnp.exp(scores - log_total)
    attended = (
        jnp.einsum(
            "hij,jhd->ihd",
            attention.astype(jnp.bfloat16),
            value_heads,
            preferred_element_type=jnp.float32,
        )
        .reshape(row_count, features)
        .astype(jnp.bfloat16)
    )
    middle = inputs + jnp.dot(attended, output_w, preferred_element_type=jnp.float32)
    scale_two = lax.rsqrt(jnp.mean(middle * middle, axis=1, keepdims=True) + epsilon)
    normed_two = middle * scale_two
    gain_two_f = gain_two.astype(jnp.float32)
    moe_in = (normed_two * gain_two_f).astype(jnp.bfloat16)
    logits = jnp.dot(moe_in, router_w, preferred_element_type=jnp.float32)
    chosen = jnp.take_along_axis(logits, routes, axis=1)
    gate_weights = jax.nn.softmax(chosen, axis=1)
    slots = capacity_slots(routes, expert_count)
    places = routes * capacity + slots
    flat_places = places.reshape(-1)
    outgoing = (
        jnp.zeros((expert_count * capacity, features), jnp.bfloat16)
        .at[flat_places]
        .set(jnp.repeat(moe_in, 2, axis=0))
    )
    arrived = to_owners(outgoing, expert_count, capacity, features)
    pre_active = jnp.einsum("erd,edf->erf", arrived, w_in, preferred_element_type=jnp.float32)
    active_full, gelu_back = jax.vjp(gelu_tanh, pre_active)
    active = active_full.astype(jnp.bfloat16)
    partial_rows = jnp.einsum("erf,efd->erd", active, w_out, preferred_element_type=jnp.float32)
    returned = from_owners(partial_rows, expert_count, capacity, features)
    picked = returned[places].astype(jnp.float32)
    outputs = middle + jnp.sum(gate_weights[:, :, None] * picked, axis=1)
    result = outputs.astype(jnp.bfloat16)
    grad_out = cotangent.astype(jnp.float32)
    slot_grads = (gate_weights[:, :, None] * grad_out[:, None, :]).astype(jnp.bfloat16)
    grad_outgoing = (
        jnp.zeros((expert_count * capacity, features), jnp.bfloat16)
        .at[flat_places]
        .set(slot_grads.reshape(-1, features))
    )
    grad_gates = jnp.sum(grad_out[:, None, :] * picked, axis=2)
    grad_arrived = to_owners(grad_outgoing, expert_count, capacity, features)
    grad_active = jnp.einsum(
        "erd,efd->erf", grad_arrived, w_out, preferred_element_type=jnp.float32
    )
    grad_pre = gelu_back(grad_active)[0].astype(jnp.bfloat16)
    grad_w_out = jnp.einsum(
        "erf,erd->efd", active, grad_arrived, preferred_element_type=jnp.float32
    )
    grad_w_in = jnp.einsum("erd,erf->edf", arrived, grad_pre, preferred_element_type=jnp.float32)
    grad_partial = jnp.einsum("erf,edf->erd", grad_pre, w_in, preferred_element_type=jnp.float32)
    grad_returned = from_owners(grad_partial, expert_count, capacity, features)
    gate_mix = jnp.sum(gate_weights * grad_gates, axis=1, keepdims=True)
    grad_chosen = gate_weights * (grad_gates - gate_mix)
    expert_match = (routes[:, :, None] == jnp.arange(expert_count, dtype=jnp.int32)).astype(
        jnp.float32
    )
    grad_logits = jnp.sum(grad_chosen[:, :, None] * expert_match, axis=1).astype(jnp.bfloat16)
    grad_moe = jnp.sum(grad_returned[places].astype(jnp.float32), axis=1) + jnp.dot(
        grad_logits, router_w.T, preferred_element_type=jnp.float32
    )
    grad_router = jnp.dot(moe_in.T, grad_logits, preferred_element_type=jnp.float32)
    grad_gain_two = jnp.sum(grad_moe * normed_two, axis=0)
    grad_middle = grad_out + rms_backward(grad_moe * gain_two_f, normed_two, scale_two)
    grad_branch = grad_middle.astype(jnp.bfloat16)
    grad_output_w = jnp.dot(attended.T, grad_branch, preferred_element_type=jnp.float32)
    grad_attended = (
        jnp.dot(grad_branch, output_w.T, preferred_element_type=jnp.float32)
        .astype(jnp.bfloat16)
        .reshape(head_shape)
    )
    attention = jnp.exp(scores_of() - log_total)
    grad_values = (
        jnp.einsum(
            "hij,ihd->jhd",
            attention.astype(jnp.bfloat16),
            grad_attended,
            preferred_element_type=jnp.float32,
        )
        .astype(jnp.bfloat16)
        .reshape(row_count, features)
    )
    grad_attention = jnp.einsum(
        "ihd,jhd->hij", grad_attended, value_heads, preferred_element_type=jnp.float32
    )
    grad_scores = (
        attention * (grad_attention - jnp.sum(attention * grad_attention, axis=2, keepdims=True))
    ).astype(jnp.bfloat16)
    grad_bias = jnp.einsum("hij,ijb->hb", grad_scores, onehot, preferred_element_type=jnp.float32)
    grad_queries = (
        (
            jnp.einsum("hij,jhd->ihd", grad_scores, key_heads, preferred_element_type=jnp.float32)
            * score_scale
        )
        .astype(jnp.bfloat16)
        .reshape(row_count, features)
    )
    grad_keys = (
        (
            jnp.einsum("hij,ihd->jhd", grad_scores, query_heads, preferred_element_type=jnp.float32)
            * score_scale
        )
        .astype(jnp.bfloat16)
        .reshape(row_count, features)
    )
    grad_query_w = jnp.dot(hidden_one.T, grad_queries, preferred_element_type=jnp.float32)
    grad_key_w = jnp.dot(hidden_one.T, grad_keys, preferred_element_type=jnp.float32)
    grad_value_w = jnp.dot(hidden_one.T, grad_values, preferred_element_type=jnp.float32)
    grad_hidden = jnp.dot(grad_queries, query_w.T, preferred_element_type=jnp.float32)
    grad_hidden = grad_hidden + jnp.dot(grad_keys, key_w.T, preferred_element_type=jnp.float32)
    grad_hidden = grad_hidden + jnp.dot(grad_values, value_w.T, preferred_element_type=jnp.float32)
    grad_gain_one = jnp.sum(grad_hidden * normed_one, axis=0)
    grad_tokens = grad_middle + rms_backward(grad_hidden * gain_one_f, normed_one, scale_one)
    local_grads = (
        grad_gain_one,
        grad_query_w,
        grad_key_w,
        grad_value_w,
        grad_output_w,
        grad_bias,
        grad_gain_two,
        grad_router,
    )
    sliced = (
        *tuple(
            (
                part.astype(jnp.float32)
                for part in side_by_side(
                    (
                        local_grads[0].astype(jnp.bfloat16),
                        local_grads[1].astype(jnp.bfloat16),
                        local_grads[2].astype(jnp.bfloat16),
                        local_grads[3].astype(jnp.bfloat16),
                        local_grads[4].astype(jnp.bfloat16),
                    ),
                    "shard",
                    0,
                    1,
                )
            )
        ),
        lax.psum_scatter(
            local_grads[5].astype(jnp.bfloat16), "shard", scatter_dimension=0, tiled=True
        ).astype(jnp.float32),
        *tuple(
            (
                part.astype(jnp.float32)
                for part in side_by_side(
                    (local_grads[6].astype(jnp.bfloat16), local_grads[7].astype(jnp.bfloat16)),
                    "shard",
                    0,
                    1,
                )
            )
        ),
    )
    totals = tuple(
        (
            part.astype(jnp.float32)
            for part in in_one(
                (
                    sliced[0].astype(jnp.bfloat16),
                    sliced[1].astype(jnp.bfloat16),
                    sliced[2].astype(jnp.bfloat16),
                    sliced[3].astype(jnp.bfloat16),
                    sliced[4].astype(jnp.bfloat16),
                    sliced[5].astype(jnp.bfloat16),
                    sliced[6].astype(jnp.bfloat16),
                    sliced[7].astype(jnp.bfloat16),
                ),
                "expert",
            )
        )
    )
    return (
        result,
        grad_tokens,
        totals[0],
        totals[1],
        totals[2],
        totals[3],
        totals[4],
        totals[5],
        totals[6],
        totals[7],
        grad_w_in,
        grad_w_out,
    )


def solution(mesh):
    placed = (
        P(("expert", "shard"), None),
        P(("expert", "shard"), None),
        P(("expert", "shard"), None),
        P("shard"),
        P("shard", None),
        P("shard", None),
        P("shard", None),
        P("shard", None),
        P("shard", None),
        P("shard"),
        P("shard", None),
        P("expert", None, "shard"),
        P("expert", "shard", None),
        P(("expert", "shard"), None),
    )
    return jax.shard_map(
        shards,
        mesh=mesh,
        in_specs=placed,
        out_specs=(
            P(("expert", "shard"), None),
            P(("expert", "shard"), None),
            P("shard"),
            P("shard", None),
            P("shard", None),
            P("shard", None),
            P("shard", None),
            P("shard", None),
            P("shard"),
            P("shard", None),
            P("expert", None, "shard"),
            P("expert", "shard", None),
        ),
        check_vma=False,
    )
```

profile of v0, /device:TPU:1, one launch (start us, length us, event | category | flops | bytes accessed | tf_op | source)
XLA Modules:
  0.0 533.7 jit_solution(13926038138224003604)
XLA Ops:
  8.2 3.6 concatenate.15
  11.9 8.5 %all-gather = bf16[4,3,32]{2,1,0:T(4,128)(2,1)S(1)} all-gather(bf16[1,3,32]{2,1,0:T(4,128)(2,1)S(1)} %bitcast.113), channel_id=1, replica_groups=mesh['expert'=32,'shard'=4] {'shard'}, dimensions={0}, use_global_device_ids=true | all-gather | bytes 960 | tf_op jit(solution)/shard_map/all_gather | solution.py:134
  23.1 10.4 %all-gather.1 = bf16[4,192,65]{1,2,0:T(8,128)(2,1)S(1)} all-gather(bf16[1,192,65]{1,2,0:T(8,128)(2,1)S(1)} %maximum_bitcast_fusion), channel_id=1, replica_groups=mesh['expert'=32,'shard'=4] {'shard'}, dimensions={0}, use_global_device_ids=true | all-gather | bytes 124800 | tf_op jit(solution)/shard_map/all_gather | solution.py:19
  37.2 33.0 %all-gather.4.cloned.1.call-done = bf16[768,3073]{1,0:T(8,128)(2,1)} async-done(((bf16[192,3073]{1,0:T(8,128)(2,1)}), bf16[768,3073]{1,0:T(8,128)(2,1)}) %all-gather.4.cloned.1.call-update) | async-done | bytes 4720144 | tf_op jit(solution)/shard_map/all_gather | solution.py:19
  78.7 2.6 convolution_convert_fusion.11
  84.2 2.1 multiply_reduce_fusion.5
  90.7 2.9 scatter_custom_fusion
  93.6 2.1 broadcast_in_dim.41
  95.7 3.0 broadcast_in_dim.42
  98.7 9.5 %all-to-all-start = ((bf16[256,6,768]{2,1,0:T(8,128)(2,1)}), bf16[256,6,768]{2,1,0:T(8,128)(2,1)}, u32[]{:S(2)}, u32[]{:S(2)}) async-start(bf16[256,6,768]{2,1,0:T(8,128)(2,1)} %bitcast.92), calls=%async_computation | async-start | bytes 6291456 | tf_op jit(solution)/shard_map/all_to_all | solution.py:89
  110.2 2.5 mul.228
  119.4 3.1 scatter_custom_fusion.1
  122.5 2.1 broadcast_in_dim.44
  124.6 25.4 %all-to-all-done = bf16[256,6,768]{2,1,0:T(8,128)(2,1)} async-done(((bf16[256,6,768]{2,1,0:T(8,128)(2,1)}), bf16[256,6,768]{2,1,0:T(8,128)(2,1)}, u32[]{:S(2)}, u32[]{:S(2)}) %all-to-all-start) | async-done | bytes 2359328 | tf_op jit(solution)/shard_map/all_to_all | solution.py:89
  150.0 3.0 broadcast_in_dim.45
  153.0 4.7 all-to-all-start.2
  157.7 5.2 copy.251
  162.9 6.7 %copy.241 = bf16[2,768,768]{1,2,0:T(8,128)(2,1)} copy(bf16[2,768,768]{2,0,1:T(2,128)(2,1)} %bitcast.94) | data formatting | bytes 4718592 | tf_op jit(solution)/shard_map/all_to_all | solution.py:89
  169.6 4.6 fusion.71
  174.2 2.2 copy-done.28
  176.4 2.3 convolution_convert_fusion.1
  178.7 3.8 copy.220
  182.5 17.2 %all-to-all-done.2 = bf16[256,6,768]{2,1,0:T(8,128)(2,1)} async-done(((bf16[256,6,768]{2,1,0:T(8,128)(2,1)}), bf16[256,6,768]{2,1,0:T(8,128)(2,1)}, u32[]{:S(2)}, u32[]{:S(2)}) %all-to-all-start.2) | async-done | bytes 2359328 | tf_op jit(solution)/shard_map/all_to_all | solution.py:89
  199.8 5.3 all-to-all-start.1
  205.1 3.9 copy.253
  209.0 4.4 fusion.6
  213.5 2.0 convolution_convert_fusion
  215.5 3.8 copy.227
  219.4 19.1 %all-to-all-done.1 = bf16[2,768,768]{2,0,1:T(2,128)(2,1)} async-done(((bf16[2,768,768]{2,0,1:T(2,128)(2,1)}), bf16[2,768,768]{2,0,1:T(2,128)(2,1)}, u32[]{:S(2)}, u32[]{:S(2)}) %all-to-all-start.1) | async-done | bytes 2359328 | tf_op jit(solution)/shard_map/all_to_all | solution.py:103
  238.5 4.7 all-to-all-start.3
  243.7 4.5 reduce
  250.2 2.1 multiply_reduce_fusion.1
  253.2 23.7 %all-to-all-done.3 = bf16[2,768,768]{2,0,1:T(2,128)(2,1)} async-done(((bf16[2,768,768]{2,0,1:T(2,128)(2,1)}), bf16[2,768,768]{2,0,1:T(2,128)(2,1)}, u32[]{:S(2)}, u32[]{:S(2)}) %all-to-all-start.3) | async-done | bytes 2359328 | tf_op jit(solution)/shard_map/all_to_all | solution.py:103
  276.8 4.5 reduce.1
  292.4 2.5 convolution_convert_fusion.2
  296.5 2.1 fusion.27
  298.6 2.1 convolution_add_fusion.1
  300.7 2.9 fusion.42
  305.1 26.2 %concatenate.17 = bf16[768,3073]{0,1:T(8,128)(2,1)} concatenate(bf16[768,1]{0,1:T(2,128)(2,1)S(1)} %convert_element_type.312, bf16[768,768]{0,1:T(8,128)(2,1)} %convolution_convert_fusion.4, bf16[768,768]{0,1:T(8,128)(2,1)} %convolution_convert_fusion.3, bf16[768,768]{0,1:T(8,128)(2,1)} %convolution_convert_fusion.2, bf16[768,768]{0,1:T(8,128)(2,1)S(1)} %convolution_convert_fusion.5), dimensions={1} | concatenate | bytes 9440256 | tf_op jit(solution)/shard_map/concatenate | solution.py:28
  331.3 7.3 %copy.254 = bf16[768,3073]{1,0:T(8,128)(2,1)} copy(bf16[768,3073]{0,1:T(8,128)(2,1)} %concatenate.17) | data formatting | bytes 9440256
  340.5 9.2 %fusion.9 = f32[2,768,768]{2,1,0:T(8,128)} fusion(bf16[2,768,768]{2,0,1:T(2,128)(2,1)} %bitcast.96, f32[2,768,768]{2,1,0:T(8,128)} %copy-done.28), kind=kOutput, calls=%fused_computation.19 | convolution fusion | flops 1822556160 | bytes 11796480 | tf_op jit(solution)/shard_map/erf,erd->efd/dot_general | solution.py:225
  350.5 7.1 %all-reduce = bf16[12,32]{1,0:T(8,128)(2,1)S(1)} all-reduce(bf16[12,32]{1,0:T(8,128)(2,1)S(1)} %fusion.20), channel_id=3, replica_groups=mesh['expert'=32,'shard'=4] {'shard'}, use_global_device_ids=true, to_apply=%region_24.25.clone | all-reduce | flops 384 | bytes 1536
  359.7 26.9 %reduce-scatter.7.cloned.1.call-done = bf16[192,3073]{1,0:T(8,128)(2,1)} async-done(((bf16[768,3073]{1,0:T(8,128)(2,1)}), bf16[192,3073]{1,0:T(8,128)(2,1)}) %reduce-scatter.7.cloned.1.call-update) | async-done | bytes 1180048
  390.5 18.2 %concatenate.19 = bf16[602592]{0:T(1024)(128)(2,1)} concatenate(bf16[192]{0:T(256)(128)(2,1)S(1)} %slice_reduce_fusion.1, bf16[147456]{0:T(1024)(128)(2,1)S(1)} %reshape.387, bf16[147456]{0:T(1024)(128)(2,1)S(1)} %reshape.388, bf16[147456]{0:T(1024)(128)(2,1)S(1)} %reshape.389, bf16[147456]{0:T(1024)(128)(2,1)S(1)} %reshape.390, bf16[96]{0:T(256)(128)(2,1)S(1)} %reshape.391, ...), dimensions={0} | concatenate | bytes 2410368 | tf_op jit(solution)/shard_map/concatenate | solution.py:42
  408.7 6.6 %fusion.72 = f32[2,768,768]{2,1,0:T(8,128)} fusion(bf16[2,768,768]{1,2,0:T(8,128)(2,1)} %copy.241, bf16[2,768,768]{2,1,0:T(8,128)(2,1)} %copy-done.30), kind=kOutput, calls=%fused_computation.147 | convolution fusion | flops 1811939328 | bytes 9437184 | tf_op jit(solution)/shard_map/erd,erf->edf/dot_general | solution.py:228
  416.2 97.3 %all-reduce.3.cloned.1.call-done = bf16[602592]{0:T(1024)(128)(2,1)} async-done(((bf16[602592]{0:T(1024)(128)(2,1)}), bf16[602592]{0:T(1024)(128)(2,1)}) %all-reduce.3.cloned.1.call-update) | async-done | bytes 1205200 | tf_op jit(solution)/shard_map/psum | solution.py:42
  513.5 2.8 slice_convert_fusion
  516.4 2.1 reshape.396
  (183 shorter events, 65.8 us)
Async XLA Ops:
  7.2 169.2 %copy-start = (bf16[2,768,768]{2,1,0:T(8,128)(2,1)S(1)}, bf16[2,768,768]{2,1,0:T(8,128)(2,1)}, u32[]{:S(2)}) copy-start(bf16[2,768,768]{2,1,0:T(8,128)(2,1)} %param.27) | copy-start | bytes 7077892
  7.2 13.3 %copy-start.23 = (s32[31]{0:T(128)S(1)}, s32[31]{0:T(128)}, u32[]{:S(2)}) copy-start(s32[31]{0:T(128)} %constant.76.clone) | copy-start | bytes 376
  7.2 4.7 copy-start.22
  7.2 63.0 %all-gather.4.cloned.1.call-start = ((), (), s32[]{:S(2)}) async-start(), calls=%async_computation.6 | async-start | bytes 6144000 | tf_op jit(solution)/shard_map/all_gather | solution.py:19
  11.8 11.3 %copy-start.25 = (bf16[192]{0:T(256)(128)(2,1)S(1)}, bf16[192]{0:T(256)(128)(2,1)}, u32[]{:S(2)}) copy-start(bf16[192]{0:T(256)(128)(2,1)} %param.24) | copy-start | bytes 1156
  11.8 11.3 %copy-start.21 = (bf16[192,64]{0,1:T(8,128)(2,1)S(1)}, bf16[192,64]{0,1:T(8,128)(2,1)}, u32[]{:S(2)}) copy-start(bf16[192,64]{0,1:T(8,128)(2,1)} %param.25) | copy-start | bytes 73732
  11.8 21.9 %copy-start.20 = (s32[128,2]{0,1:T(2,128)S(1)}, s32[128,2]{0,1:T(2,128)}, u32[]{:S(2)}) copy-start(s32[128,2]{0,1:T(2,128)} %param.17) | copy-start | bytes 3076
  20.8 0.6 copy-start.18
  34.2 2.5 copy-start.26
  34.2 2.8 copy-start.2
  84.2 2.2 copy-start.8
  86.3 0.8 copy-start.3
  87.2 0.7 copy-start.5
  98.7 51.2 %all-to-all-start = ((bf16[256,6,768]{2,1,0:T(8,128)(2,1)}), bf16[256,6,768]{2,1,0:T(8,128)(2,1)}, u32[]{:S(2)}, u32[]{:S(2)}) async-start(bf16[256,6,768]{2,1,0:T(8,128)(2,1)} %bitcast.92), calls=%async_computation | async-start | bytes 6291456 | tf_op jit(solution)/shard_map/all_to_all | solution.py:89
  153.0 46.8 %all-to-all-start.2 = ((bf16[256,6,768]{2,1,0:T(8,128)(2,1)}), bf16[256,6,768]{2,1,0:T(8,128)(2,1)}, u32[]{:S(2)}, u32[]{:S(2)}) async-start(bf16[256,6,768]{2,1,0:T(8,128)(2,1)} %bitcast.93), calls=%async_computation.2 | async-start | bytes 6291456 | tf_op jit(solution)/shard_map/all_to_all | solution.py:89
  174.2 2.2 copy-start.28
  199.8 38.7 %all-to-all-start.1 = ((bf16[2,768,768]{2,0,1:T(2,128)(2,1)}), bf16[2,768,768]{2,0,1:T(2,128)(2,1)}, u32[]{:S(2)}, u32[]{:S(2)}) async-start(bf16[2,768,768]{2,0,1:T(2,128)(2,1)} %copy.220), calls=%async_computation.1 | async-start | bytes 4718592 | tf_op jit(solution)/shard_map/all_to_all | solution.py:103
  205.1 3.9 copy-start.29
  209.0 4.5 copy-start.7
  209.0 4.5 copy-start.24
  213.5 2.0 copy-start.30
  219.4 24.1 %copy-start.10 = (bf16[128,768]{1,0:T(8,128)(2,1)S(1)}, bf16[128,768]{1,0:T(8,128)(2,1)}, u32[]{:S(2)}) copy-start(bf16[128,768]{1,0:T(8,128)(2,1)} %param.28) | copy-start | bytes 589828
  238.5 38.3 %all-to-all-start.3 = ((bf16[2,768,768]{2,0,1:T(2,128)(2,1)}), bf16[2,768,768]{2,0,1:T(2,128)(2,1)}, u32[]{:S(2)}, u32[]{:S(2)}) async-start(bf16[2,768,768]{2,0,1:T(2,128)(2,1)} %copy.227), calls=%async_computation.3 | async-start | bytes 4718592 | tf_op jit(solution)/shard_map/all_to_all | solution.py:103
  243.2 114.6 %reduce-scatter.9.cloned.1.call-start = ((), (), s32[]{:S(2)}) async-start(), calls=%async_computation.9 | async-start | bytes 245760
  248.5 1.6 copy-start.15
  249.7 2.6 copy-start.6
  281.6 2.5 copy-start.4
  283.2 3.1 copy-start.9
  286.3 4.0 copy-start.11
  289.2 1.6 copy-start.12
  290.3 0.9 copy-start.13
  290.3 1.2 copy-start.16
  292.3 94.3 %reduce-scatter.7.cloned.1.call-start = ((), (), s32[]{:S(2)}) async-start(), calls=%async_computation.8 | async-start | bytes 6144000
  296.5 4.2 copy-start.14
  338.6 0.7 copy-start.27
  338.6 175.0 %all-reduce.3.cloned.1.call-start = ((), (), s32[]{:S(2)}) async-start(), calls=%async_computation.7 | async-start | bytes 2412544 | tf_op jit(solution)/shard_map/psum | solution.py:42
  340.4 9.6 %copy-start.19 = (s32[128,128]{1,0:T(8,128)S(1)}, s32[128,128]{1,0:T(8,128)}, u32[]{:S(2)}) copy-start(s32[128,128]{1,0:T(8,128)} %copy-done.18) | copy-start | bytes 196612
  408.7 6.6 %copy-start.17 = (f32[128,768]{1,0:T(8,128)S(1)}, f32[128,768]{1,0:T(8,128)}, u32[]{:S(2)}) copy-start(f32[128,768]{1,0:T(8,128)} %get-tuple-element.99) | copy-start | bytes 1179652
  516.4 10.3 %copy-start.1 = (bf16[2,768,768]{2,1,0:T(8,128)(2,1)S(1)}, bf16[2,768,768]{2,1,0:T(8,128)(2,1)}, u32[]{:S(2)}) copy-start(bf16[2,768,768]{2,1,0:T(8,128)(2,1)} %param.27) | copy-start | bytes 7077892
Sparse Core Ops, SparseCore 0:
  11.9 58.2 all-gather.3
  292.5 13.1 reduce-scatter.8
  338.7 47.8 reduce-scatter.6
  408.8 104.7 all-reduce.2
where the time goes:
time: 543 us; the launch traced here: 534 us
  waiting for transfers between devices  243 us (45%)
  local copies, waits for them, and re-layouts  137 us (25%)
  matrix products  61.3 us (11%)
  blocking collectives  26.1 us (5%)
  other arithmetic  26 us (5%)
  starting transfers between devices  24.5 us (5%)
  between operations  15.7 us (3%)
    psum x1, waiting for transfers between devices, in_one(): so_far = lax.psum(jnp.concatenate([a.ravel() for a in arrays]), axis)  97.3 us
    all_to_all x2, waiting for transfers between devices, from_owners(): lax.all_to_all(partial_rows.astype(jnp.bfloat16), ('expert', 'shard'), sp...  42.8 us
    all_to_all x2, waiting for transfers between devices, to_owners(): lax.all_to_all(fanned.reshape(expert_ranks * shard_ranks * local_count, c...  42.6 us
    all_gather x1, waiting for transfers between devices, sent_together(): result = lax.all_gather(both, axis, axis=dim, tiled=True)  33 us
    unnamed x6, waiting for transfers between devices  27 us
    concatenate x1, local copies, waits for them, and re-layouts, side_by_side(): jnp.concatenate([a.reshape(*a.shape[:along], w) for a, w in zip(arrays, w...  26.2 us
    concatenate x1, local copies, waits for them, and re-layouts, in_one(): so_far = lax.psum(jnp.concatenate([a.ravel() for a in arrays]), axis)  18.2 us
    all_to_all x3, local copies, waits for them, and re-layouts, to_owners(): lax.all_to_all(fanned.reshape(expert_ranks * shard_ranks * local_count, c...  15.8 us
  transfers between devices with their start and end apart: 8, of which 7 were waited for; matrix products, arithmetic and copies ran while one was open for 25% of the time, Pallas kernels for 0%

commit v1 on v0

v1 whole, which is shorter than its diff:
```python
import math

import jax
import jax.numpy as jnp
from jax import lax
from jax.experimental import pallas as pl
from jax.experimental.pallas import tpu as pltpu
from jax.sharding import Mesh, PartitionSpec as P

epsilon = 1e-06
bucket_edges = list(range(1, 17)) + [
    int(math.ceil(16.0 * 8.0 ** ((bucket_level - 16) / 16.0))) for bucket_level in range(17, 32)
]


def row_segments(lengths, row_count):
    sequence_ends = jnp.cumsum(lengths)
    positions = jnp.arange(row_count, dtype=jnp.int32)
    return jnp.sum((positions[:, None] >= sequence_ends[None, :]).astype(jnp.int32), axis=1)


def position_tables(row_count, bucket_count):
    positions = jnp.arange(row_count, dtype=jnp.int32)
    distance = positions[:, None] - positions[None, :]
    edge_values = jnp.array(bucket_edges, dtype=jnp.int32)
    bucket = jnp.sum((distance[:, :, None] >= edge_values).astype(jnp.int32), axis=2)
    onehot = (bucket[:, :, None] == jnp.arange(bucket_count, dtype=jnp.int32)).astype(jnp.bfloat16)
    return (distance, onehot)


def capacity_slots(route_block, expert_count):
    order_block = jnp.arange(route_block.shape[0], dtype=jnp.int32)
    named_rows = jnp.sum(
        (route_block[:, :, None] == jnp.arange(expert_count, dtype=jnp.int32)).astype(jnp.bfloat16),
        axis=1,
    )
    earlier = (order_block[None, :] < order_block[:, None]).astype(jnp.bfloat16)
    counts = jnp.dot(earlier, named_rows, preferred_element_type=jnp.float32)
    match = route_block[:, :, None] == jnp.arange(expert_count, dtype=jnp.int32)
    return jnp.sum(jnp.where(match, counts[:, None, :], 0.0), axis=2).astype(jnp.int32)


def gelu_tanh(argument):
    return jax.nn.gelu(argument, approximate=True)


def rms_backward(grad_normed, normed, scale):
    return scale * (grad_normed - normed * jnp.mean(grad_normed * normed, axis=1, keepdims=True))


def shift_x(block, step):
    ranks = lax.axis_size("x")
    return lax.ppermute(block, "x", [(i, (i + step) % ranks) for i in range(ranks)])


def swap_core(block):
    return lax.ppermute(block, "c", [(0, 1), (1, 0)])


def along_x(block):
    return [block, shift_x(block, 1), shift_x(block, 2), shift_x(block, 3)]


def pack_kernel(core_ref, *refs):
    mats, out, sems = refs[:4], refs[4], refs[5]
    half = mats[0].shape[0] // 2
    start = pl.multiple_of(core_ref[0] * half, half)
    copies = [
        pltpu.make_async_copy(m.at[pl.ds(start, half)], out.at[pl.ds(k * half, half)], sems.at[k])
        for k, m in enumerate(mats)
    ]
    for c in copies:
        c.start()
    for c in copies:
        c.wait()


def assemble_kernel(place_ref, *refs):
    mats, near, far, outs, sems = refs[:4], refs[4:7], refs[7], refs[8:12], refs[12]
    shard, core = place_ref[0], place_ref[1]
    rows = mats[0].shape[0]
    half = rows // 2
    copies = []
    for k in range(4):
        begin = pl.multiple_of(shard * rows, rows)
        copies.append((mats[k], outs[k].at[pl.ds(begin, rows)]))
    for r in range(1, 4):
        begin = lax.rem(shard + (4 - r), 4) * rows
        mine = pl.multiple_of(begin + core * half, half)
        other = pl.multiple_of(begin + (1 - core) * half, half)
        for k in range(4):
            part = pl.ds(k * half, half)
            copies.append((near[r - 1].at[part], outs[k].at[pl.ds(mine, half)]))
            part = pl.ds(((r - 1) * 4 + k) * half, half)
            copies.append((far.at[part], outs[k].at[pl.ds(other, half)]))
    copies = [pltpu.make_async_copy(s, d, sems.at[i]) for i, (s, d) in enumerate(copies)]
    for c in copies:
        c.start()
    for c in copies:
        c.wait()


ANYWHERE = pl.BlockSpec(memory_space=pl.ANY)
SCALARS = pl.BlockSpec(memory_space=pltpu.SMEM)
WHOLE = pl.BlockSpec(memory_space=pltpu.VMEM)
ROOM = pltpu.CompilerParams(vmem_limit_bytes=56 * 1024 * 1024)


def gather_weights(mats):
    shard = lax.axis_index("x").astype(jnp.int32)
    core = lax.axis_index("c").astype(jnp.int32)
    rows, cols = mats[0].shape
    half = rows // 2
    sent = pl.pallas_call(
        pack_kernel,
        out_shape=jax.ShapeDtypeStruct((4 * half, cols), jnp.bfloat16),
        in_specs=[SCALARS] + [ANYWHERE] * 4,
        out_specs=ANYWHERE,
        scratch_shapes=[pltpu.SemaphoreType.DMA((4,))],
        name="pack",
    )(core[None], *mats)
    near = along_x(sent)[1:]
    far = swap_core(jnp.concatenate(near, axis=0))
    full = jax.ShapeDtypeStruct((4 * rows, cols), jnp.bfloat16)
    return pl.pallas_call(
        assemble_kernel,
        out_shape=[full] * 4,
        in_specs=[SCALARS] + [ANYWHERE] * 8,
        out_specs=[ANYWHERE] * 4,
        scratch_shapes=[pltpu.SemaphoreType.DMA((28,))],
        name="assemble",
    )(jnp.stack([shard, core]), *mats, *near, far)


def dispatch_kernel(places_ref, *refs):
    pieces, out_ref = refs[:4], refs[4]
    rows = out_ref.shape[0]
    features = 768
    wide = pieces[0].shape[1] > features
    tokens = pieces[0].shape[0]
    line = jnp.concatenate([p[...] for p in pieces], axis=0)
    places = places_ref[...]
    row = lax.broadcasted_iota(jnp.int32, (rows, 4 * tokens), 0)
    for e in range(2):
        at = row + e * rows
        pick = ((at == places[0:1]) | (at == places[1:2])).astype(jnp.float32).astype(jnp.bfloat16)
        out_ref[:, e * features : (e + 1) * features] = jnp.dot(
            pick, line[:, :features], preferred_element_type=jnp.float32
        ).astype(jnp.bfloat16)
        if wide:
            ids = jnp.dot(pick, line[:, features:], preferred_element_type=jnp.float32)
            if e == 0:
                extra = ids
            else:
                extra = extra + pltpu.roll(ids, 2, axis=1)
    if wide:
        out_ref[:, 2 * features :] = extra.astype(jnp.bfloat16)


def dispatch(places, pieces, rows):
    features = 768
    lanes = 2 * features + pieces[0].shape[1] - features
    return pl.pallas_call(
        dispatch_kernel,
        out_shape=jax.ShapeDtypeStruct((rows, lanes), jnp.bfloat16),
        in_specs=[WHOLE] * 5,
        out_specs=WHOLE,
        compiler_params=ROOM,
        name="dispatch",
    )(places, *pieces)


def chosen_logit(logits, ids):
    lanes = lax.broadcasted_iota(jnp.int32, logits.shape, 1)
    return jnp.sum(jnp.where(lanes == ids, logits, 0.0), axis=1, keepdims=True)


def gate_pair(first, second):
    top = jnp.maximum(first, second)
    one, two = jnp.exp(first - top), jnp.exp(second - top)
    total = one + two
    return one / total, two / total


def expert_kernel(
    own_ref, x_ref, g_ref, ids_ref, in_ref, out_ref, router_ref, ret_ref, act_ref, pre_ref, arr_ref
):
    f32, bf16 = jnp.float32, jnp.bfloat16
    e = pl.program_id(0)
    own = own_ref[0] + e
    features = x_ref.shape[1]
    step = 256
    slope = math.sqrt(2.0 / math.pi)
    last = (((1,), (1,)), ((), ()))

    def chunk(i, carry):
        at = pl.ds(pl.multiple_of(i * step, step), step)
        x = x_ref[at, :]
        ids = ids_ref[at, :].astype(f32)
        lanes = lax.broadcasted_iota(jnp.int32, ids.shape, 1)
        mine = (lanes == 2 * e) | (lanes == 2 * e + 1)
        other = jnp.sum(jnp.where(mine, ids, 0.0), axis=1, keepdims=True).astype(jnp.int32) - own
        logits = jnp.dot(x, router_ref[...], preferred_element_type=f32)
        gate, _ = gate_pair(chosen_logit(logits, own), chosen_logit(logits, other))
        pre = jnp.dot(x, in_ref[0], preferred_element_type=f32)
        tanh = jnp.tanh(slope * (pre + 0.044715 * (pre * pre * pre)))
        active = (0.5 * pre * (1.0 + tanh)).astype(bf16)
        act_ref[0, at, :] = active
        ret_ref[at, :features] = jnp.dot(active, out_ref[0], preferred_element_type=f32).astype(bf16)
        rows = (gate * g_ref[at, :].astype(f32)).astype(bf16)
        arr_ref[0, at, :] = rows
        back = lax.dot_general(rows, out_ref[0], last, preferred_element_type=f32)
        rise = 0.5 * (1.0 + tanh) + 0.5 * pre * (1.0 - tanh * tanh) * (
            slope * (1.0 + 3.0 * 0.044715 * (pre * pre))
        )
        grad = (back * rise).astype(bf16)
        pre_ref[0, at, :] = grad
        ret_ref[at, features:] = lax.dot_general(
            grad, in_ref[0], last, preferred_element_type=f32
        ).astype(bf16)
        return carry

    lax.fori_loop(0, x_ref.shape[0] // step, chunk, 0)


def experts(own, arrived, grad_wide, w_in, w_out, router_w):
    rows = arrived.shape[0]
    features = w_in.shape[1]
    hidden = w_in.shape[2]
    bf16 = jnp.bfloat16
    per = lambda n: pl.BlockSpec((rows, n), lambda e: (0, e))
    weights = lambda a, b: pl.BlockSpec((1, a, b), lambda e: (e, 0, 0))
    return pl.pallas_call(
        expert_kernel,
        grid=(2,),
        out_shape=[
            jax.ShapeDtypeStruct((rows, 4 * features), bf16),
            jax.ShapeDtypeStruct((2, rows, hidden), bf16),
            jax.ShapeDtypeStruct((2, rows, hidden), bf16),
            jax.ShapeDtypeStruct((2, rows, features), bf16),
        ],
        in_specs=[
            SCALARS,
            per(features),
            per(features),
            pl.BlockSpec((rows, 128), lambda e: (0, 2 * features // 128)),
            weights(features, hidden),
            weights(hidden, features),
            pl.BlockSpec(router_w.shape, lambda e: (0, 0)),
        ],
        out_specs=[
            per(2 * features),
            weights(rows, hidden),
            weights(rows, hidden),
            weights(rows, features),
        ],
        compiler_params=ROOM,
        name="experts",
    )(own[None], arrived, grad_wide, grad_wide, w_in, w_out, router_w)


def combine_kernel(places_ref, routes_ref, router_ref, ret_ref, *refs):
    f32, bf16 = jnp.float32, jnp.bfloat16
    grads, moes, outs = refs[:4], refs[4:8], refs[8:12]
    tokens = moes[0].shape[0]
    features = moes[0].shape[1]
    rows = ret_ref.shape[0]
    lane = lax.broadcasted_iota(jnp.int32, (tokens, rows), 1)
    tail_lane = lax.broadcasted_iota(jnp.int32, (tokens, 128), 1)
    for r in range(4):
        here = slice(r * tokens, (r + 1) * tokens)
        logits = jnp.dot(moes[r][...], router_ref[...], preferred_element_type=f32)
        gates = gate_pair(
            chosen_logit(logits, routes_ref[here, 0:1]), chosen_logit(logits, routes_ref[here, 1:2])
        )
        total = jnp.zeros((tokens, features), f32)
        back = jnp.zeros((tokens, features), f32)
        tail = jnp.zeros((tokens, 128), f32)
        grad = grads[r][:, :features].astype(f32)
        picks = [
            [
                (lane + e * rows == places_ref[here, k : k + 1]).astype(f32).astype(bf16)
                for e in range(2)
            ]
            for k in range(2)
        ]
        for k in range(2):
            got = jnp.zeros((tokens, features), f32)
            for e in range(2):
                at = 2 * e * features
                got = got + jnp.dot(
                    picks[k][e], ret_ref[:, at : at + features], preferred_element_type=f32
                )
            total = total + gates[k] * got
            dots = jnp.sum(grad * got, axis=1, keepdims=True)
            high = dots.astype(bf16).astype(f32)
            tail = jnp.where(tail_lane == k, high, tail)
            tail = jnp.where(tail_lane == 2 + k, dots - high, tail)
        for e in range(2):
            at = (2 * e + 1) * features
            back = back + jnp.dot(
                picks[0][e] + picks[1][e],
                ret_ref[:, at : at + features],
                preferred_element_type=f32,
            )
        outs[r][:, :features] = total.astype(bf16)
        outs[r][:, features : 2 * features] = back.astype(bf16)
        outs[r][:, 2 * features :] = tail.astype(bf16)


def combine(places, routes, router_w, returned, grads, moes):
    tokens, features = moes[0].shape
    return pl.pallas_call(
        combine_kernel,
        out_shape=[jax.ShapeDtypeStruct((tokens, 2 * features + 128), jnp.bfloat16)] * 4,
        in_specs=[WHOLE] * 12,
        out_specs=[WHOLE] * 4,
        compiler_params=ROOM,
        name="combine",
    )(places, routes, router_w, returned, *grads, *moes)


def layer(
    tokens,
    seq_lengths,
    routes,
    gain_attn,
    w_query,
    w_key,
    w_value,
    w_output,
    rel_bias,
    gain_moe,
    w_router,
    w_in,
    w_out,
    cotangent,
):
    row_count, features = tokens.shape
    shard_rows = w_query.shape[0]
    expert_count = w_router.shape[1]
    bucket_count = rel_bias.shape[1]
    head_count = 4 * rel_bias.shape[0]
    head_size = features // head_count
    capacity = 3 * row_count // expert_count
    score_scale = 1.0 / math.sqrt(head_size)
    head_shape = (row_count, head_count, head_size)
    bias_size = rel_bias.size
    f32 = jnp.float32
    bf16 = jnp.bfloat16

    small = jnp.concatenate(
        [
            w_router,
            gain_attn[:, None],
            gain_moe[:, None],
            jnp.pad(rel_bias.reshape(-1), (0, shard_rows - bias_size))[:, None],
            jnp.zeros((shard_rows, 128 - expert_count - 3), bf16),
        ],
        axis=1,
    )
    query_w, key_w, value_w, output_w = gather_weights((w_query, w_key, w_value, w_output))
    shard = lax.axis_index("x")
    rest = jnp.take(jnp.stack(along_x(small)), (shard - jnp.arange(4)) % 4, axis=0)
    router_w = rest[:, :, :expert_count].reshape(features, expert_count)
    gain_one = rest[:, :, expert_count].reshape(features)
    gain_two = rest[:, :, expert_count + 1].reshape(features)
    bias_table = rest[:, :bias_size, expert_count + 2].reshape(head_count, bucket_count)

    route_rows = jnp.pad(routes.astype(bf16), ((0, 0), (0, 126)))
    line_grads = along_x(jnp.concatenate([cotangent, route_rows], axis=1))
    line_routes = jnp.concatenate(
        [piece[:, features : features + 2] for piece in line_grads], axis=0
    ).astype(jnp.int32)
    line_slots = jnp.concatenate(
        [
            capacity_slots(line_routes[r * row_count : (r + 1) * row_count], expert_count)
            + r * capacity
            for r in range(4)
        ],
        axis=0,
    )
    owners = expert_count // 2
    group = 4 * capacity
    slot_rows = owners * group
    line_places = (line_routes % 2) * slot_rows + (line_routes // 2) * group + line_slots

    def to_owners(pieces):
        return lax.all_to_all(
            dispatch(line_places.T, pieces, slot_rows), ("y", "z", "c"), 0, 0, tiled=True
        )

    grad_wide = to_owners(line_grads)
    first_expert = 2 * lax.axis_index(("y", "z", "c")).astype(jnp.int32)

    inputs = tokens.astype(f32)
    scale_one = lax.rsqrt(jnp.mean(inputs * inputs, axis=1, keepdims=True) + epsilon)
    normed_one = inputs * scale_one
    gain_one_f = gain_one.astype(f32)
    hidden_one = (normed_one * gain_one_f).astype(bf16)
    queries = jnp.dot(hidden_one, query_w, preferred_element_type=f32).astype(bf16)
    key_rows = jnp.dot(hidden_one, key_w, preferred_element_type=f32).astype(bf16)
    value_rows = jnp.dot(hidden_one, value_w, preferred_element_type=f32).astype(bf16)
    query_heads = queries.reshape(head_shape)
    key_heads = key_rows.reshape(head_shape)
    value_heads = value_rows.reshape(head_shape)
    segments = row_segments(seq_lengths[0], row_count)
    distance, onehot = position_tables(row_count, bucket_count)
    allowed = (segments[:, None] == segments[None, :]) & (distance >= 0)
    position_bias = jnp.einsum("ijb,hb->hij", onehot, bias_table, preferred_element_type=f32)

    def scores_of():
        raw_scores = (
            jnp.einsum("ihd,jhd->hij", query_heads, key_heads, preferred_element_type=f32)
            * score_scale
            + position_bias
        )
        return jnp.where(allowed[None], raw_scores, -1000000000.0)

    scores = scores_of()
    row_max = jnp.max(scores, axis=2, keepdims=True)
    log_total = row_max + jnp.log(jnp.sum(jnp.exp(scores - row_max), axis=2, keepdims=True))
    attention = jnp.exp(scores - log_total)
    attended = (
        jnp.einsum("hij,jhd->ihd", attention.astype(bf16), value_heads, preferred_element_type=f32)
        .reshape(row_count, features)
        .astype(bf16)
    )
    middle = inputs + jnp.dot(attended, output_w, preferred_element_type=f32)
    scale_two = lax.rsqrt(jnp.mean(middle * middle, axis=1, keepdims=True) + epsilon)
    normed_two = middle * scale_two
    gain_two_f = gain_two.astype(f32)
    moe_in = (normed_two * gain_two_f).astype(bf16)

    line_moe = along_x(moe_in)
    arrived = to_owners(line_moe)
    ret, active, grad_pre, grad_arrived = experts(
        first_expert, arrived, grad_wide, w_in, w_out, router_w
    )
    returned = lax.all_to_all(ret, ("y", "z", "c"), 0, 0, tiled=True)
    grad_w_out = jnp.einsum("erf,erd->efd", active, grad_arrived, preferred_element_type=f32)
    grad_w_in = jnp.einsum(
        "red,erf->edf",
        arrived.reshape(slot_rows, 2, features),
        grad_pre,
        preferred_element_type=f32,
    )

    bundle = combine(line_places, line_routes, router_w, returned, line_grads, line_moe)
    home = bundle[0][:, : 2 * features + 4].astype(f32)
    for r in range(1, 4):
        home = home + shift_x(bundle[r], -r)[:, : 2 * features + 4].astype(f32)
    outputs = middle + home[:, :features]
    result = outputs.astype(bf16)
    grad_gates = home[:, 2 * features : 2 * features + 2] + home[:, 2 * features + 2 :]
    logits = jnp.dot(moe_in, router_w, preferred_element_type=f32)
    lanes = jnp.arange(expert_count, dtype=jnp.int32)
    gate_weights = jax.nn.softmax(
        jnp.sum(jnp.where(routes[:, :, None] == lanes, logits[:, None, :], 0.0), axis=2), axis=1
    )
    grad_out = cotangent.astype(f32)
    gate_mix = jnp.sum(gate_weights * grad_gates, axis=1, keepdims=True)
    grad_chosen = gate_weights * (grad_gates - gate_mix)
    expert_match = (routes[:, :, None] == jnp.arange(expert_count, dtype=jnp.int32)).astype(f32)
    grad_logits = jnp.sum(grad_chosen[:, :, None] * expert_match, axis=1).astype(bf16)
    grad_moe = home[:, features : 2 * features] + jnp.dot(
        grad_logits, router_w.T, preferred_element_type=f32
    )
    grad_router = jnp.dot(moe_in.T, grad_logits, preferred_element_type=f32)
    grad_gain_two = jnp.sum(grad_moe * normed_two, axis=0)
    grad_middle = grad_out + rms_backward(grad_moe * gain_two_f, normed_two, scale_two)
    grad_branch = grad_middle.astype(bf16)
    grad_output_w = jnp.dot(attended.T, grad_branch, preferred_element_type=f32)
    grad_attended = (
        jnp.dot(grad_branch, output_w.T, preferred_element_type=f32).astype(bf16).reshape(head_shape)
    )
    grad_values = (
        jnp.einsum(
            "hij,ihd->jhd", attention.astype(bf16), grad_attended, preferred_element_type=f32
        )
        .astype(bf16)
        .reshape(row_count, features)
    )
    grad_attention = jnp.einsum(
        "ihd,jhd->hij", grad_attended, value_heads, preferred_element_type=f32
    )
    grad_scores = (
        attention * (grad_attention - jnp.sum(attention * grad_attention, axis=2, keepdims=True))
    ).astype(bf16)
    grad_bias = jnp.einsum("hij,ijb->hb", grad_scores, onehot, preferred_element_type=f32)
    grad_queries = (
        (
            jnp.einsum("hij,jhd->ihd", grad_scores, key_heads, preferred_element_type=f32)
            * score_scale
        )
        .astype(bf16)
        .reshape(row_count, features)
    )
    grad_keys = (
        (
            jnp.einsum("hij,ihd->jhd", grad_scores, query_heads, preferred_element_type=f32)
            * score_scale
        )
        .astype(bf16)
        .reshape(row_count, features)
    )
    grad_query_w = jnp.dot(hidden_one.T, grad_queries, preferred_element_type=f32)
    grad_key_w = jnp.dot(hidden_one.T, grad_keys, preferred_element_type=f32)
    grad_value_w = jnp.dot(hidden_one.T, grad_values, preferred_element_type=f32)
    grad_hidden = jnp.dot(grad_queries, query_w.T, preferred_element_type=f32)
    grad_hidden = grad_hidden + jnp.dot(grad_keys, key_w.T, preferred_element_type=f32)
    grad_hidden = grad_hidden + jnp.dot(grad_values, value_w.T, preferred_element_type=f32)
    grad_gain_one = jnp.sum(grad_hidden * normed_one, axis=0)
    grad_tokens = grad_middle + rms_backward(grad_hidden * gain_one_f, normed_one, scale_one)

    core = lax.axis_index("c")
    piece = shard_rows // 8
    wide = features + 128
    bias_column = jnp.pad(grad_bias.reshape(4, bias_size), ((0, 0), (0, shard_rows - bias_size)))
    small_grads = jnp.concatenate(
        [
            grad_router,
            grad_gain_one[:, None],
            grad_gain_two[:, None],
            bias_column.reshape(-1, 1),
        ],
        axis=1,
    ).astype(bf16)
    small_grads = jnp.pad(small_grads, ((0, 0), (0, 128 - small_grads.shape[1])))
    none = jnp.zeros_like(small_grads)
    stacked = jnp.stack(
        [
            jnp.concatenate([g.astype(bf16), s], axis=1)
            for g, s in (
                (grad_query_w, small_grads),
                (grad_key_w, none),
                (grad_value_w, none),
                (grad_output_w, none),
            )
        ]
    ).reshape(4, 4, 4, 2, piece, wide)
    kept = lax.dynamic_index_in_dim(stacked, core, 3, keepdims=False)
    given = lax.dynamic_index_in_dim(stacked, 1 - core, 3, keepdims=False)
    paired = (kept.astype(f32) + swap_core(given).astype(f32)).astype(bf16)
    paired = paired.transpose(0, 2, 1, 3, 4).reshape(64 * piece, wide)
    spread = lax.all_to_all(paired, ("y", "z", "x"), 0, 0, tiled=True)
    mine = jnp.sum(spread.reshape(64, piece, wide).astype(f32), axis=0).astype(bf16)
    totals = lax.all_to_all(
        jnp.broadcast_to(mine[None], (32, piece, wide)).reshape(32 * piece, wide),
        ("y", "z", "c"),
        0,
        0,
        tiled=True,
    ).reshape(4, shard_rows, wide)
    small_totals = totals[0, :, features:].astype(f32)
    totals = totals[:, :, :features].astype(f32)
    router_total = small_totals[:, :expert_count]
    gain_one_total = small_totals[:, expert_count]
    gain_two_total = small_totals[:, expert_count + 1]
    bias_total = small_totals[:bias_size, expert_count + 2].reshape(rel_bias.shape)
    return (
        result,
        grad_tokens,
        gain_one_total,
        totals[0],
        totals[1],
        totals[2],
        totals[3],
        bias_total,
        gain_two_total,
        router_total,
        grad_w_in,
        grad_w_out,
    )


def solution(mesh):
    cube = Mesh(mesh.devices.reshape(4, 4, 2, 4), ("y", "z", "c", "x"))
    expert = ("y", "z", "c")
    everyone = ("y", "z", "c", "x")
    placed = (
        P(everyone, None),
        P(everyone, None),
        P(everyone, None),
        P("x"),
        P("x", None),
        P("x", None),
        P("x", None),
        P("x", None),
        P("x", None),
        P("x"),
        P("x", None),
        P(expert, None, "x"),
        P(expert, "x", None),
        P(everyone, None),
    )
    return jax.shard_map(
        layer,
        mesh=cube,
        in_specs=placed,
        out_specs=(
            P(everyone, None),
            P(everyone, None),
            P("x"),
            P("x", None),
            P("x", None),
            P("x", None),
            P("x", None),
            P("x", None),
            P("x"),
            P("x", None),
            P(expert, None, "x"),
            P(expert, "x", None),
        ),
        check_vma=False,
    )
```

time: 543 us -> 537 us (0.989)
  Pallas kernels: 0 us -> 196 us
  local copies, waits for them, and re-layouts: 137 us -> 38.4 us
  waiting for transfers between devices: 243 us -> 182 us
  starting transfers between devices: 24.5 us -> 58.4 us
  matrix products: 61.3 us -> 34.3 us
  blocking collectives: 26.1 us -> 0 us
  between operations: 15.7 us -> 2.05 us
  other arithmetic: 26 us -> 16.2 us
    pallas_call x0 -> x6, Pallas kernels: none -> 196 us  [the longest x1 145 us: gather_weights(): pl.pallas_call(assemble_kernel, out_shape=[full] * 4, in_specs=[SCALARS]...]
    psum x1 -> x0, waiting for transfers between devices: 97.3 us -> none  [in_one(): so_far = lax.psum(jnp.concatenate([a.ravel() for a in arrays]), axis)]
    ppermute x0 -> x17, waiting for transfers between devices: none -> 56.1 us  [the longest x15 51.1 us: shift_x(): lax.ppermute(block, 'x', [(i, (i + step) % ranks) for i in range(ranks)])]
    concatenate x3 -> x6, local copies, waits for them, and re-layouts: 48 us -> 3.72 us  [the longest x4 2.58 us: layer(): jnp.concatenate([g.astype(bf16), s], axis=1)]
    all_to_all x4 -> x5, waiting for transfers between devices: 85.4 us -> 126 us  [the longest x1 58.2 us: layer(): returned = lax.all_to_all(ret, ('y', 'z', 'c'), 0, 0, tiled=True)]
    all_gather x1 -> x0, waiting for transfers between devices: 33 us -> none  [sent_together(): result = lax.all_gather(both, axis, axis=dim, tiled=True)]
    dot_general x29 -> x28, matrix products: 59.7 us -> 32.5 us  [the longest x1 6.77 us: layer(): jnp.einsum('erf,erd->efd', active, grad_arrived, preferred_element_type=f32)]
    unnamed x6 -> x0, waiting for transfers between devices: 27 us -> none
  transfers between devices with their start and end apart: 8 -> 22, of which waited for: 7 -> 13; matrix products, arithmetic and copies ran while one was open for 25% -> 8% of each run, Pallas kernels for 0% -> 33%
where the time goes in v1:
time: 537 us; the launch traced here: 528 us
  Pallas kernels  196 us (36%)
  waiting for transfers between devices  182 us (34%)
  starting transfers between devices  58.4 us (11%)
  local copies, waits for them, and re-layouts  38.4 us (7%)
  matrix products  34.3 us (6%)
  other arithmetic  16.2 us (3%)
    pallas_call x1, Pallas kernels, gather_weights(): pl.pallas_call(assemble_kernel, out_shape=[full] * 4, in_specs=[SCALARS]...  145 us
    all_to_all x1, waiting for transfers between devices, layer(): returned = lax.all_to_all(ret, ('y', 'z', 'c'), 0, 0, tiled=True)  58.2 us
    ppermute x15, waiting for transfers between devices, shift_x(): lax.ppermute(block, 'x', [(i, (i + step) % ranks) for i in range(ranks)])  51.1 us
    all_to_all x1, waiting for transfers between devices, layer(): spread = lax.all_to_all(paired, ('y', 'z', 'x'), 0, 0, tiled=True)  30.2 us
    all_to_all x2, waiting for transfers between devices, to_owners(): lax.all_to_all(dispatch(line_places.T, pieces, slot_rows), ('y', 'z', 'c'...  29.4 us
    ppermute x15, starting transfers between devices, shift_x(): lax.ppermute(block, 'x', [(i, (i + step) % ranks) for i in range(ranks)])  19.8 us
    pallas_call x1, Pallas kernels, gather_weights(): pl.pallas_call(pack_kernel, out_shape=jax.ShapeDtypeStruct((4 * half, col...  19 us
    all_to_all x2, starting transfers between devices, to_owners(): lax.all_to_all(dispatch(line_places.T, pieces, slot_rows), ('y', 'z', 'c'...  16.3 us
  transfers between devices with their start and end apart: 22, of which 13 were waited for; matrix products, arithmetic and copies ran while one was open for 8% of the time, Pallas kernels for 33%

profile of v1, /device:TPU:1, one launch (start us, length us, event | category | flops | bytes accessed | tf_op | source)
XLA Modules:
  0.0 528.1 jit_solution(1617498396581318264)
XLA Ops:
  2.4 2.1 collective-permute-start.7
  4.5 2.5 collective-permute-start.8
  10.1 2.3 collective-permute-start.1
  17.2 19.0 %pack.1 = bf16[384,768]{1,0:T(8,128)(2,1)} custom-call(s32[1]{0:T(128)} %bitcast.6.core_ref, bf16[192,768]{1,0:T(8,128)(2,1)} %refs_0_.3, bf16[192,768]{1,0:T(8,128)(2,1)} %refs_1_.3, bf16[192,768]{1,0:T(8,128)(2,1)} %refs_2_.3, bf16[192,768]{1,0:T(8,128)(2,1)} %refs_3_.3), custom_call_target="tpu_custom_call" | custom-call | tf_op jit(solution)/shard_map/pack/pallas_call | solution.py:114
  37.7 2.4 collective-permute-start.4
  46.1 5.0 collective-permute-done.3.refs_4_
  51.1 12.8 %collective-permute-done.4.refs_5_ = bf16[384,768]{1,0:T(8,128)(2,1)S(1)} collective-permute-done((bf16[384,768]{1,0:T(8,128)(2,1)}, bf16[384,768]{1,0:T(8,128)(2,1)S(1)}, u32[]{:S(2)}, u32[]{:S(2)}) %collective-permute-start.4) | collective-permute-done | bytes 589856 | tf_op jit(solution)/shard_map/ppermute | solution.py:53
  64.0 4.2 collective-permute-done.5.refs_6_
  72.8 4.6 dispatch.3
  77.5 8.2 %all-to-all-start.1 = ((bf16[32,24,1664]{2,1,0:T(8,128)(2,1)}), bf16[32,24,1664]{2,1,0:T(8,128)(2,1)S(1)}, u32[]{:S(2)}, u32[]{:S(2)}) async-start(bf16[32,24,1664]{2,1,0:T(8,128)(2,1)} %bitcast.110), calls=%async_computation.1 | async-start | bytes 5111808 | tf_op jit(solution)/shard_map/all_to_all | solution.py:389
  85.7 145.1 %assemble.1 = (bf16[768,768]{1,0:T(8,128)(2,1)}, bf16[768,768]{1,0:T(8,128)(2,1)}, bf16[768,768]{1,0:T(8,128)(2,1)}, bf16[768,768]{1,0:T(8,128)(2,1)}) custom-call(s32[2]{0:T(128)} %pad_add_fusion.1.place_ref, bf16[192,768]{1,0:T(8,128)(2,1)} %refs_0_.3, bf16[192,768]{1,0:T(8,128)(2,1)} %refs_1_.3, bf16[192,768]{1,0:T(8,128)(2,1)} %refs_2_.3, ...), custom_call_target="tpu_custom_call" | custom-call | tf_op jit(solution)/shard_map/assemble/pallas_call | solution.py:125
  230.8 1.6 convolution_convert_fusion.8
  233.3 1.6 convolution_convert_fusion.7
  235.7 1.6 convolution_convert_fusion.9
  238.2 1.8 fusion.81
  243.0 2.4 collective-permute-start.11
  246.5 2.8 collective-permute-done.10.refs_1_.refs_5_
  249.3 5.1 collective-permute-done.11.refs_2_.refs_6_
  255.7 4.1 dispatch.2
  259.8 1.5 copy-done
  261.3 8.1 %all-to-all-start = ((bf16[32,24,1536]{2,1,0:T(8,128)(2,1)}), bf16[32,24,1536]{2,1,0:T(8,128)(2,1)}, u32[]{:S(2)}, u32[]{:S(2)}) async-start(bf16[32,24,1536]{2,1,0:T(8,128)(2,1)} %bitcast.111), calls=%async_computation | async-start | bytes 4718592 | tf_op jit(solution)/shard_map/all_to_all | solution.py:389
  271.2 29.4 %all-to-all-done = bf16[32,24,1536]{2,1,0:T(8,128)(2,1)} async-done(((bf16[32,24,1536]{2,1,0:T(8,128)(2,1)}), bf16[32,24,1536]{2,1,0:T(8,128)(2,1)}, u32[]{:S(2)}, u32[]{:S(2)}) %all-to-all-start) | async-done | bytes 2359328 | tf_op jit(solution)/shard_map/all_to_all | solution.py:389
  300.6 15.4 %experts.1 = (bf16[768,3072]{1,0:T(8,128)(2,1)}, bf16[2,768,768]{2,1,0:T(8,128)(2,1)}, bf16[2,768,768]{2,1,0:T(8,128)(2,1)}, bf16[2,768,768]{2,1,0:T(8,128)(2,1)}) custom-call(s32[1]{0:T(128)} %bitcast.15.own_ref, bf16[768,1536]{1,0:T(8,128)(2,1)} %bitcast.18.x_ref, bf16[768,1664]{1,0:T(8,128)(2,1)} %bitcast.107, bf16[768,1664]{1,0:T(8,128)(2,1)} %bitcast.108, ...), custom_call_target="tpu_custom_call" | custom-call | tf_op jit(solution)/shard_map/experts/pallas_call | solution.py:233
  316.0 5.5 %all-to-all-start.2 = ((bf16[32,24,3072]{2,1,0:T(8,128)(2,1)}), bf16[32,24,3072]{2,1,0:T(8,128)(2,1)}, u32[]{:S(2)}, u32[]{:S(2)}) async-start(bf16[32,24,3072]{2,1,0:T(8,128)(2,1)} %bitcast.122), calls=%async_computation.2 | async-start | bytes 9437184 | tf_op jit(solution)/shard_map/all_to_all | solution.py:440
  321.8 58.2 %all-to-all-done.2 = bf16[32,24,3072]{2,1,0:T(8,128)(2,1)} async-done(((bf16[32,24,3072]{2,1,0:T(8,128)(2,1)}), bf16[32,24,3072]{2,1,0:T(8,128)(2,1)}, u32[]{:S(2)}, u32[]{:S(2)}) %all-to-all-start.2) | async-done | bytes 4718624 | tf_op jit(solution)/shard_map/all_to_all | solution.py:440
  380.1 8.1 %combine.1 = (bf16[128,1664]{1,0:T(8,128)(2,1)}, bf16[128,1664]{1,0:T(8,128)(2,1)}, bf16[128,1664]{1,0:T(8,128)(2,1)}, bf16[128,1664]{1,0:T(8,128)(2,1)}) custom-call(s32[512,2]{1,0:T(8,128)} %copy-done.19, s32[512,2]{1,0:T(8,128)} %copy-done.18, bf16[768,64]{1,0:T(8,128)(2,1)} %bitcast.119, bf16[768,3072]{1,0:T(8,128)(2,1)} %bitcast.22.ret_ref, ...), custom_call_target="tpu_custom_call" | custom-call | tf_op jit(solution)/shard_map/combine/pallas_call | solution.py:313
  388.2 1.5 collective-permute-start.13
  391.1 8.0 %collective-permute-done.13 = bf16[128,1664]{1,0:T(8,128)(2,1)S(1)} collective-permute-done((bf16[128,1664]{1,0:T(8,128)(2,1)}, bf16[128,1664]{1,0:T(8,128)(2,1)S(1)}, u32[]{:S(2)}, u32[]{:S(2)}) %collective-permute-start.13) | collective-permute-done | bytes 426016 | tf_op jit(solution)/shard_map/ppermute | solution.py:53
  399.1 2.6 collective-permute-done.14
  401.8 10.5 %collective-permute-done.15 = bf16[128,1664]{1,0:T(8,128)(2,1)S(1)} collective-permute-done((bf16[128,1664]{1,0:T(8,128)(2,1)}, bf16[128,1664]{1,0:T(8,128)(2,1)S(1)}, u32[]{:S(2)}, u32[]{:S(2)}) %collective-permute-start.15) | collective-permute-done | bytes 426016 | tf_op jit(solution)/shard_map/ppermute | solution.py:53
  415.5 1.9 multiply_reduce_fusion.1
  417.5 1.9 multiply_add_fusion
  425.4 1.6 convolution_convert_fusion.3
  427.0 1.5 convolution_convert_fusion.1
  429.0 1.6 convolution_convert_fusion.2
  431.2 1.8 fusion.26
  434.7 1.5 concatenate.39
  437.6 2.0 dynamic-slice_bitcast_fusion
  441.3 4.9 collective-permute-done.16
  446.2 2.5 fusion.1
  448.7 1.8 copy.197
  450.5 8.0 %all-to-all-start.3 = ((bf16[64,24,896]{2,1,0:T(8,128)(2,1)}), bf16[64,24,896]{2,1,0:T(8,128)(2,1)S(1)}, u32[]{:S(2)}, u32[]{:S(2)}) async-start(bf16[64,24,896]{2,1,0:T(8,128)(2,1)} %bitcast.109), calls=%async_computation.3 | async-start | bytes 5505024 | tf_op jit(solution)/shard_map/all_to_all | solution.py:546
  458.5 6.0 %reshape.308 = bf16[768,2,768]{2,1,0:T(2,128)(2,1)} reshape(bf16[32,24,1536]{2,1,0:T(8,128)(2,1)} %all-to-all-done) | data formatting | bytes 4718592 | tf_op jit(solution)/shard_map/reshape | solution.py:444
  464.5 30.2 %all-to-all-done.3 = bf16[64,24,896]{2,1,0:T(8,128)(2,1)S(1)} async-done(((bf16[64,24,896]{2,1,0:T(8,128)(2,1)}), bf16[64,24,896]{2,1,0:T(8,128)(2,1)S(1)}, u32[]{:S(2)}, u32[]{:S(2)}) %all-to-all-start.3) | async-done | bytes 2752544 | tf_op jit(solution)/shard_map/all_to_all | solution.py:546
  496.2 6.9 %all-to-all-start.4 = ((bf16[32,24,896]{2,1,0:T(8,128)(2,1)}), bf16[32,24,896]{2,1,0:T(8,128)(2,1)S(1)}, u32[]{:S(2)}, u32[]{:S(2)}) async-start(bf16[32,24,896]{2,1,0:T(8,128)(2,1)} %broadcast_in_dim.93), calls=%async_computation.4 | async-start | bytes 2752512 | tf_op jit(solution)/shard_map/all_to_all | solution.py:548
  503.2 6.8 %fusion.85 = f32[2,768,768]{2,1,0:T(8,128)} fusion(bf16[2,768,768]{2,1,0:T(8,128)(2,1)} %get-tuple-element.34, bf16[2,768,768]{2,1,0:T(8,128)(2,1)} %get-tuple-element.35), kind=kOutput, calls=%fused_computation.176 | convolution fusion | flops 1811939328 | bytes 9437184 | tf_op jit(solution)/shard_map/erf,erd->efd/dot_general | solution.py:441
  510.0 4.2 fusion.2
  515.1 8.5 %all-to-all-done.4 = bf16[32,24,896]{2,1,0:T(8,128)(2,1)S(1)} async-done(((bf16[32,24,896]{2,1,0:T(8,128)(2,1)}), bf16[32,24,896]{2,1,0:T(8,128)(2,1)S(1)}, u32[]{:S(2)}, u32[]{:S(2)}) %all-to-all-start.4) | async-done | bytes 1376288 | tf_op jit(solution)/shard_map/all_to_all | solution.py:548
  (242 shorter events, 54.2 us)
Async XLA Ops:
  2.4 39.7 %copy-start.24 = (bf16[128,896]{1,0:T(8,128)(2,1)}, bf16[128,896]{1,0:T(8,128)(2,1)S(1)}, u32[]{:S(2)}) copy-start(bf16[128,896]{1,0:T(8,128)(2,1)S(1)} %fusion.41.refs_0_) | copy-start | bytes 688132
  2.4 41.0 %collective-permute-start.7 = (bf16[128,896]{1,0:T(8,128)(2,1)S(1)}, bf16[128,896]{1,0:T(8,128)(2,1)S(1)}, u32[]{:S(2)}, u32[]{:S(2)}) collective-permute-start(bf16[128,896]{1,0:T(8,128)(2,1)S(1)} %fusion.41.refs_0_), channel_id=1, source_target_pairs={{0,1},{1,2},{2,3},{3,0},{4,5},{5,6},{6,7},{7,4},{8,9},{9,10},{10,1... | collective-permute-start | bytes 688136 | tf_op jit(solution)/shard_map/ppermute | solution.py:53
  4.5 40.1 %collective-permute-start.8 = (bf16[128,896]{1,0:T(8,128)(2,1)S(1)}, bf16[128,896]{1,0:T(8,128)(2,1)S(1)}, u32[]{:S(2)}, u32[]{:S(2)}) collective-permute-start(bf16[128,896]{1,0:T(8,128)(2,1)S(1)} %fusion.41.refs_0_), channel_id=1, source_target_pairs={{0,2},{1,3},{2,0},{3,1},{4,6},{5,7},{6,4},{7,5},{8,10},{9,11},{10,... | collective-permute-start | bytes 688136 | tf_op jit(solution)/shard_map/ppermute | solution.py:53
  10.1 26.1 %collective-permute-start = (bf16[192,128]{0,1:T(8,128)(2,1)S(1)}, bf16[192,128]{0,1:T(8,128)(2,1)S(1)}, u32[]{:S(2)}, u32[]{:S(2)}) collective-permute-start(bf16[192,128]{0,1:T(8,128)(2,1)S(1)} %concatenate.32), channel_id=1, source_target_pairs={{0,1},{1,2},{2,3},{3,0},{4,5},{5,6},{6,7},{7,4},{8,9},{9,10},{10,1... | collective-permute-start | bytes 147464 | tf_op jit(solution)/shard_map/ppermute | solution.py:53
  10.1 26.8 %collective-permute-start.1 = (bf16[192,128]{0,1:T(8,128)(2,1)S(1)}, bf16[192,128]{0,1:T(8,128)(2,1)S(1)}, u32[]{:S(2)}, u32[]{:S(2)}) collective-permute-start(bf16[192,128]{0,1:T(8,128)(2,1)S(1)} %concatenate.32), channel_id=1, source_target_pairs={{0,2},{1,3},{2,0},{3,1},{4,6},{5,7},{6,4},{7,5},{8,10},{9,11},{10,... | collective-permute-start | bytes 147464 | tf_op jit(solution)/shard_map/ppermute | solution.py:53
  12.5 25.3 %collective-permute-start.2 = (bf16[192,128]{0,1:T(8,128)(2,1)S(1)}, bf16[192,128]{0,1:T(8,128)(2,1)S(1)}, u32[]{:S(2)}, u32[]{:S(2)}) collective-permute-start(bf16[192,128]{0,1:T(8,128)(2,1)S(1)} %concatenate.32), channel_id=1, source_target_pairs={{0,3},{1,0},{2,1},{3,2},{4,7},{5,4},{6,5},{7,6},{8,11},{9,8},{10,9... | collective-permute-start | bytes 147464 | tf_op jit(solution)/shard_map/ppermute | solution.py:53
  13.9 221.8 %copy-start.44 = (f32[128]{0:T(128)}, f32[128]{0:T(128)S(1)}, u32[]{:S(2)}) copy-start(f32[128]{0:T(128)S(1)} %add_rsqrt_fusion.1) | copy-start | bytes 1540
  16.6 25.5 %copy-start.42 = (s32[128,128]{1,0:T(8,128)}, s32[128,128]{1,0:T(8,128)S(1)}, u32[]{:S(2)}) copy-start(s32[128,128]{1,0:T(8,128)S(1)} %convert_reduce_fusion) | copy-start | bytes 196612
  36.2 8.4 %collective-permute-start.9 = (bf16[128,896]{1,0:T(8,128)(2,1)S(1)}, bf16[128,896]{1,0:T(8,128)(2,1)S(1)}, u32[]{:S(2)}, u32[]{:S(2)}) collective-permute-start(bf16[128,896]{1,0:T(8,128)(2,1)S(1)} %fusion.41.refs_0_), channel_id=1, source_target_pairs={{0,3},{1,0},{2,1},{3,2},{4,7},{5,4},{6,5},{7,6},{8,11},{9,8},{10,9... | collective-permute-start | bytes 688136 | tf_op jit(solution)/shard_map/ppermute | solution.py:53
  36.9 14.2 %collective-permute-start.3 = (bf16[384,768]{1,0:T(8,128)(2,1)}, bf16[384,768]{1,0:T(8,128)(2,1)S(1)}, u32[]{:S(2)}, u32[]{:S(2)}) collective-permute-start(bf16[384,768]{1,0:T(8,128)(2,1)} %pack.1), channel_id=1, source_target_pairs={{0,1},{1,2},{2,3},{3,0},{4,5},{5,6},{6,7},{7,4},{8,9},{9,10},{10,1... | collective-permute-start | bytes 1769480 | tf_op jit(solution)/shard_map/ppermute | solution.py:53
  37.7 26.2 %collective-permute-start.4 = (bf16[384,768]{1,0:T(8,128)(2,1)}, bf16[384,768]{1,0:T(8,128)(2,1)S(1)}, u32[]{:S(2)}, u32[]{:S(2)}) collective-permute-start(bf16[384,768]{1,0:T(8,128)(2,1)} %pack.1), channel_id=1, source_target_pairs={{0,2},{1,3},{2,0},{3,1},{4,6},{5,7},{6,4},{7,5},{8,10},{9,11},{10,... | collective-permute-start | bytes 1769480 | tf_op jit(solution)/shard_map/ppermute | solution.py:53
  43.4 26.2 %copy-start.33 = (bf16[128,896]{1,0:T(8,128)(2,1)}, bf16[128,896]{1,0:T(8,128)(2,1)S(1)}, u32[]{:S(2)}) copy-start(bf16[128,896]{1,0:T(8,128)(2,1)S(1)} %collective-permute-done.7.refs_1_) | copy-start | bytes 688132
  43.4 24.7 %collective-permute-start.5 = (bf16[384,768]{1,0:T(8,128)(2,1)}, bf16[384,768]{1,0:T(8,128)(2,1)S(1)}, u32[]{:S(2)}, u32[]{:S(2)}) collective-permute-start(bf16[384,768]{1,0:T(8,128)(2,1)} %pack.1), channel_id=1, source_target_pairs={{0,3},{1,0},{2,1},{3,2},{4,7},{5,4},{6,5},{7,6},{8,11},{9,8},{10,9... | collective-permute-start | bytes 1769480 | tf_op jit(solution)/shard_map/ppermute | solution.py:53
  44.6 25.0 %copy-start.34 = (bf16[128,896]{1,0:T(8,128)(2,1)}, bf16[128,896]{1,0:T(8,128)(2,1)S(1)}, u32[]{:S(2)}) copy-start(bf16[128,896]{1,0:T(8,128)(2,1)S(1)} %collective-permute-done.8.refs_2_) | copy-start | bytes 688132
  44.6 28.2 %copy-start.35 = (bf16[128,896]{1,0:T(8,128)(2,1)}, bf16[128,896]{1,0:T(8,128)(2,1)S(1)}, u32[]{:S(2)}) copy-start(bf16[128,896]{1,0:T(8,128)(2,1)S(1)} %collective-permute-done.9.refs_3_) | copy-start | bytes 688132
  51.1 21.0 %copy-start.20 = (bf16[384,768]{1,0:T(8,128)(2,1)}, bf16[384,768]{1,0:T(8,128)(2,1)S(1)}, u32[]{:S(2)}) copy-start(bf16[384,768]{1,0:T(8,128)(2,1)S(1)} %collective-permute-done.3.refs_4_) | copy-start | bytes 1769476
  64.0 8.1 %copy-start.21 = (bf16[384,768]{1,0:T(8,128)(2,1)}, bf16[384,768]{1,0:T(8,128)(2,1)S(1)}, u32[]{:S(2)}) copy-start(bf16[384,768]{1,0:T(8,128)(2,1)S(1)} %collective-permute-done.4.refs_5_) | copy-start | bytes 1769476
  69.6 16.1 %collective-permute-start.6 = (bf16[1152,768]{1,0:T(8,128)(2,1)}, bf16[1152,768]{1,0:T(8,128)(2,1)}, u32[]{:S(2)}, u32[]{:S(2)}) collective-permute-start(bf16[1152,768]{1,0:T(8,128)(2,1)} %pad_maximum_fusion.1), channel_id=1, source_target_pairs={{0,4},{4,0},{1,5},{5,1},{2,6},{6,2},{3,7},{7,3},{8,12},{12,8},{9,1... | collective-permute-start | bytes 5308424 | tf_op jit(solution)/shard_map/ppermute | solution.py:57
  72.1 5.4 %copy-start.19 = (s32[512,2]{1,0:T(8,128)}, s32[512,2]{1,0:T(8,128)S(1)}, u32[]{:S(2)}) copy-start(s32[512,2]{1,0:T(8,128)S(1)} %fusion.35.places_ref) | copy-start | bytes 12292
  77.5 182.4 %all-to-all-start.1 = ((bf16[32,24,1664]{2,1,0:T(8,128)(2,1)}), bf16[32,24,1664]{2,1,0:T(8,128)(2,1)S(1)}, u32[]{:S(2)}, u32[]{:S(2)}) async-start(bf16[32,24,1664]{2,1,0:T(8,128)(2,1)} %bitcast.110), calls=%async_computation.1 | async-start | bytes 5111808 | tf_op jit(solution)/shard_map/all_to_all | solution.py:389
  85.7 145.1 %copy-start.2 = (bf16[128,768]{1,0:T(8,128)(2,1)S(1)}, bf16[128,768]{1,0:T(8,128)(2,1)}, u32[]{:S(2)}) copy-start(bf16[128,768]{1,0:T(8,128)(2,1)} %param.15) | copy-start | bytes 589828
  240.4 14.0 %copy-start.25 = (bf16[12,64,128]{2,1,0:T(8,128)(2,1)}, bf16[12,64,128]{2,1,0:T(8,128)(2,1)S(1)}, u32[]{:S(2)}) copy-start(bf16[12,64,128]{2,1,0:T(8,128)(2,1)S(1)} %convolution_convert_fusion.6) | copy-start | bytes 589828
  240.9 13.5 %copy-start.48 = (f32[128]{0:T(128)}, f32[128]{0:T(128)S(1)}, u32[]{:S(2)}) copy-start(f32[128]{0:T(128)S(1)} %add_rsqrt_fusion) | copy-start | bytes 1540
  241.7 12.7 %copy-start.5 = (bf16[128,768]{1,0:T(8,128)(2,1)}, bf16[128,768]{1,0:T(8,128)(2,1)S(1)}, u32[]{:S(2)}) copy-start(bf16[128,768]{1,0:T(8,128)(2,1)S(1)} %multiply_convert_fusion.1.refs_0_.refs_4_) | copy-start | bytes 589828
  241.7 7.5 %collective-permute-start.10 = (bf16[128,768]{1,0:T(8,128)(2,1)S(1)}, bf16[128,768]{1,0:T(8,128)(2,1)S(1)}, u32[]{:S(2)}, u32[]{:S(2)}) collective-permute-start(bf16[128,768]{1,0:T(8,128)(2,1)S(1)} %multiply_convert_fusion.1.refs_0_.refs_4_), channel_id=1, source_target_pairs={{0,1},{1,2},{2,3},{3,0},{4,5},{5,6},{6,7},{7,4},{8,9},{9,10},{10,1... | collective-permute-start | bytes 589832 | tf_op jit(solution)/shard_map/ppermute | solution.py:53
  243.0 11.4 %collective-permute-start.11 = (bf16[128,768]{1,0:T(8,128)(2,1)S(1)}, bf16[128,768]{1,0:T(8,128)(2,1)S(1)}, u32[]{:S(2)}, u32[]{:S(2)}) collective-permute-start(bf16[128,768]{1,0:T(8,128)(2,1)S(1)} %multiply_convert_fusion.1.refs_0_.refs_4_), channel_id=1, source_target_pairs={{0,2},{1,3},{2,0},{3,1},{4,6},{5,7},{6,4},{7,5},{8,10},{9,11},{10,... | collective-permute-start | bytes 589832 | tf_op jit(solution)/shard_map/ppermute | solution.py:53
  245.3 9.0 %collective-permute-start.12 = (bf16[128,768]{1,0:T(8,128)(2,1)S(1)}, bf16[128,768]{1,0:T(8,128)(2,1)S(1)}, u32[]{:S(2)}, u32[]{:S(2)}) collective-permute-start(bf16[128,768]{1,0:T(8,128)(2,1)S(1)} %multiply_convert_fusion.1.refs_0_.refs_4_), channel_id=1, source_target_pairs={{0,3},{1,0},{2,1},{3,2},{4,7},{5,4},{6,5},{7,6},{8,11},{9,8},{10,9... | collective-permute-start | bytes 589832 | tf_op jit(solution)/shard_map/ppermute | solution.py:53
  249.3 5.1 copy-start.36
  261.3 39.3 %all-to-all-start = ((bf16[32,24,1536]{2,1,0:T(8,128)(2,1)}), bf16[32,24,1536]{2,1,0:T(8,128)(2,1)}, u32[]{:S(2)}, u32[]{:S(2)}) async-start(bf16[32,24,1536]{2,1,0:T(8,128)(2,1)} %bitcast.111), calls=%async_computation | async-start | bytes 4718592 | tf_op jit(solution)/shard_map/all_to_all | solution.py:389
  316.0 5.5 %copy-start.6 = (bf16[128,768]{1,0:T(8,128)(2,1)S(1)}, bf16[128,768]{1,0:T(8,128)(2,1)}, u32[]{:S(2)}) copy-start(bf16[128,768]{1,0:T(8,128)(2,1)} %copy-done.5) | copy-start | bytes 589828
  316.0 5.5 %copy-start.8 = (bf16[4,192,64]{2,1,0:T(8,128)(2,1)S(1)}, bf16[4,192,64]{2,1,0:T(8,128)(2,1)}, u32[]{:S(2)}) copy-start(bf16[4,192,64]{2,1,0:T(8,128)(2,1)} %copy.185) | copy-start | bytes 294916
  316.0 64.0 %all-to-all-start.2 = ((bf16[32,24,3072]{2,1,0:T(8,128)(2,1)}), bf16[32,24,3072]{2,1,0:T(8,128)(2,1)}, u32[]{:S(2)}, u32[]{:S(2)}) async-start(bf16[32,24,3072]{2,1,0:T(8,128)(2,1)} %bitcast.122), calls=%async_computation.2 | async-start | bytes 9437184 | tf_op jit(solution)/shard_map/all_to_all | solution.py:440
  380.1 10.9 %copy-start.46 = (s32[128,2]{0,1:T(2,128)S(1)}, s32[128,2]{0,1:T(2,128)}, u32[]{:S(2)}) copy-start(s32[128,2]{0,1:T(2,128)} %param.17) | copy-start | bytes 3076
  388.2 26.5 %copy-start.7 = (bf16[128,768]{1,0:T(8,128)(2,1)S(1)}, bf16[128,768]{1,0:T(8,128)(2,1)}, u32[]{:S(2)}) copy-start(bf16[128,768]{1,0:T(8,128)(2,1)} %copy-done.5) | copy-start | bytes 589828
  388.2 27.3 %copy-start.4 = (f32[128,768]{1,0:T(8,128)S(1)}, f32[128,768]{1,0:T(8,128)}, u32[]{:S(2)}) copy-start(f32[128,768]{1,0:T(8,128)} %copy-done.3) | copy-start | bytes 1179652
  388.2 27.3 %copy-start.9 = (bf16[4,192,64]{2,1,0:T(8,128)(2,1)S(1)}, bf16[4,192,64]{2,1,0:T(8,128)(2,1)}, u32[]{:S(2)}) copy-start(bf16[4,192,64]{2,1,0:T(8,128)(2,1)} %copy.185) | copy-start | bytes 294916
  388.2 27.3 %copy-start.49 = (f32[128]{0:T(128)S(1)}, f32[128]{0:T(128)}, u32[]{:S(2)}) copy-start(f32[128]{0:T(128)} %copy-done.48) | copy-start | bytes 1540
  388.2 10.9 %collective-permute-start.13 = (bf16[128,1664]{1,0:T(8,128)(2,1)}, bf16[128,1664]{1,0:T(8,128)(2,1)S(1)}, u32[]{:S(2)}, u32[]{:S(2)}) collective-permute-start(bf16[128,1664]{1,0:T(8,128)(2,1)} %get-tuple-element.30), channel_id=1, source_target_pairs={{0,3},{1,0},{2,1},{3,2},{4,7},{5,4},{6,5},{7,6},{8,11},{9,8},{10,9... | collective-permute-start | bytes 1277960 | tf_op jit(solution)/shard_map/ppermute | solution.py:53
  389.7 12.1 %collective-permute-start.14 = (bf16[128,1664]{1,0:T(8,128)(2,1)}, bf16[128,1664]{1,0:T(8,128)(2,1)S(1)}, u32[]{:S(2)}, u32[]{:S(2)}) collective-permute-start(bf16[128,1664]{1,0:T(8,128)(2,1)} %get-tuple-element.31), channel_id=1, source_target_pairs={{0,2},{1,3},{2,0},{3,1},{4,6},{5,7},{6,4},{7,5},{8,10},{9,11},{10,... | collective-permute-start | bytes 1277960 | tf_op jit(solution)/shard_map/ppermute | solution.py:53
  390.7 21.6 %collective-permute-start.15 = (bf16[128,1664]{1,0:T(8,128)(2,1)}, bf16[128,1664]{1,0:T(8,128)(2,1)S(1)}, u32[]{:S(2)}, u32[]{:S(2)}) collective-permute-start(bf16[128,1664]{1,0:T(8,128)(2,1)} %get-tuple-element.32), channel_id=1, source_target_pairs={{0,1},{1,2},{2,3},{3,0},{4,5},{5,6},{6,7},{7,4},{8,9},{9,10},{10,1... | collective-permute-start | bytes 1277960 | tf_op jit(solution)/shard_map/ppermute | solution.py:53
  414.4 5.0 copy-start.14
  422.7 4.3 copy-start.26
  440.8 5.4 %collective-permute-start.16 = (bf16[4,4,4,24,896]{4,3,2,1,0:T(8,128)(2,1)}, bf16[4,4,4,24,896]{4,3,2,1,0:T(8,128)(2,1)S(1)}, u32[]{:S(2)}, u32[]{:S(2)}) collective-permute-start(bf16[4,4,4,24,896]{4,3,2,1,0:T(8,128)(2,1)} %dynamic-slice_bitcast_fusion), channel_id=1, source_target_pairs={{0,4},{4,0},{1,5},{5,1},{2,6},{6,2},{3,7},{7,3},{8,12},{12,8},{9,1... | collective-permute-start | bytes 8257544 | tf_op jit(solution)/shard_map/ppermute | solution.py:57
  450.5 44.2 %all-to-all-start.3 = ((bf16[64,24,896]{2,1,0:T(8,128)(2,1)}), bf16[64,24,896]{2,1,0:T(8,128)(2,1)S(1)}, u32[]{:S(2)}, u32[]{:S(2)}) async-start(bf16[64,24,896]{2,1,0:T(8,128)(2,1)} %bitcast.109), calls=%async_computation.3 | async-start | bytes 5505024 | tf_op jit(solution)/shard_map/all_to_all | solution.py:546
  496.2 27.4 %all-to-all-start.4 = ((bf16[32,24,896]{2,1,0:T(8,128)(2,1)}), bf16[32,24,896]{2,1,0:T(8,128)(2,1)S(1)}, u32[]{:S(2)}, u32[]{:S(2)}) async-start(bf16[32,24,896]{2,1,0:T(8,128)(2,1)} %broadcast_in_dim.93), calls=%async_computation.4 | async-start | bytes 2752512 | tf_op jit(solution)/shard_map/all_to_all | solution.py:548
  503.1 6.8 %copy-start.23 = (bf16[768,2,768]{2,1,0:T(2,128)(2,1)S(1)}, bf16[768,2,768]{2,1,0:T(2,128)(2,1)}, u32[]{:S(2)}) copy-start(bf16[768,2,768]{2,1,0:T(2,128)(2,1)} %reshape.308) | copy-start | bytes 7077892
  503.2 6.8 %copy-start.51 = (bf16[2,768,768]{2,1,0:T(8,128)(2,1)S(1)}, bf16[2,768,768]{2,1,0:T(8,128)(2,1)}, u32[]{:S(2)}) copy-start(bf16[2,768,768]{2,1,0:T(8,128)(2,1)} %get-tuple-element.33) | copy-start | bytes 7077892
  509.9 4.3 copy-start.32
  (26 other events, 54.0 us)
